TPU v7x, 256 devices: a whole 4x4x8 slice. The times are simulated.
256 devices in a mesh: row: 16 (over z_hi, x), col: 16 (over y, z_lo, core).
Axes of the slice: x: 4, y: 4, z: 8 (z_hi: 4, z_lo: 2; z = z_hi * 2 + z_lo), core: 2. Of those that a mesh axis runs over, the one named last changes fastest.
Arguments:
- right_side: float32 [64, 16, 4096], P(None, 'col', 'row'), may hold values from -24 to 24
- tile_values: bfloat16 [16, 16, 64, 256, 256], P('row', 'col'), may hold values from -0.5 to 0.5
- tile_rows: int32 [16, 16, 64], P('row', 'col'), may hold values from 0 to 15, as said below
- tile_cols: int32 [16, 16, 64], P('row', 'col'), may hold values from 0 to 7
- tile_count: int32 [16, 16], P('row', 'col'), may hold values from 32 to 64, as said below
Outputs:
- solution: float32 [64, 16, 2048], P(None, 'row', 'col')
- residual: float32 [64, 16, 4096], P(None, 'col', 'row')
Inputs may be any that keep to these rules, and one draw needn't show every extreme that they name: `tile_rows`: within one device no two tiles share both tile row and tile column. The first tile_count tiles of a device's list belong to the matrix, the others are ignored.
All inputs are finite; a program needn't handle non-finite values.
Results may differ from a plain program's by a relative error of at most 0.013.
Values may be sent and summed in bfloat16 or wider, within the bound.
A program may use at most 64 MiB of HBM per device.

v0:
```python
import jax
import jax.numpy as jnp
from jax import lax
from jax.sharding import PartitionSpec as P

RBG = 16
CBG = 8
ITERS = 2


EPSILON = 1e-06


def forward_part(vector, tile_set, col_pick, row_add):
    sides = vector.shape[0]
    blocks = vector.reshape(sides, col_pick.shape[1], tile_set.shape[2])
    picked = jnp.einsum("tk,rkj->trj", col_pick, blocks, preferred_element_type=jnp.float32).astype(
        jnp.bfloat16
    )
    products = jnp.einsum("tij,trj->tri", tile_set, picked, preferred_element_type=jnp.float32)
    summed = jnp.einsum("tb,tri->rbi", row_add, products, precision=lax.Precision.HIGHEST)
    return summed.reshape(sides, -1)


def backward_part(vector, tile_set, row_pick, col_add):
    sides = vector.shape[0]
    blocks = vector.reshape(sides, row_pick.shape[1], tile_set.shape[1])
    picked = jnp.einsum("tb,rbi->tri", row_pick, blocks, preferred_element_type=jnp.float32).astype(
        jnp.bfloat16
    )
    products = jnp.einsum("tij,tri->trj", tile_set, picked, preferred_element_type=jnp.float32)
    summed = jnp.einsum("tk,trj->rkj", col_add, products, precision=lax.Precision.HIGHEST)
    return summed.reshape(sides, -1)


def local(right_side, tile_values, tile_rows, tile_cols, tile_count):
    tile_set = tile_values[0, 0]
    slot_total = tile_set.shape[0]
    live_mask = (lax.iota(jnp.int32, slot_total) < tile_count[0, 0]).astype(jnp.float32)
    row_hits = tile_rows[0, 0][:, None] == lax.iota(jnp.int32, RBG)[None, :]
    col_hits = tile_cols[0, 0][:, None] == lax.iota(jnp.int32, CBG)[None, :]
    row_pick = row_hits.astype(jnp.bfloat16)
    col_pick = col_hits.astype(jnp.bfloat16)
    row_add = row_hits.astype(jnp.float32) * live_mask[:, None]
    col_add = col_hits.astype(jnp.float32) * live_mask[:, None]
    begin = right_side[:, 0, :]

    def forward(vector_low):
        whole = lax.all_gather(vector_low, "col", axis=1, tiled=True)
        return lax.psum_scatter(
            forward_part(whole, tile_set, col_pick, row_add), "row", scatter_dimension=1, tiled=True
        )

    def backward(vector_low):
        whole = lax.all_gather(vector_low, "row", axis=1, tiled=True)
        return lax.psum_scatter(
            backward_part(whole, tile_set, row_pick, col_add),
            "col",
            scatter_dimension=1,
            tiled=True,
        )

    def data_norm(vector):
        return jnp.sqrt(lax.psum(jnp.sum(vector * vector, axis=1), ("row", "col")) + EPSILON)

    def model_norm(vector):
        return jnp.sqrt(lax.psum(jnp.sum(vector * vector, axis=1), ("row", "col")) + EPSILON)

    backward_out = backward(begin.astype(jnp.bfloat16))
    beta_norm = data_norm(begin)
    right_raw = backward_out / beta_norm[:, None]
    alpha_norm = model_norm(right_raw)
    left_vector = begin / beta_norm[:, None]
    right_vector = right_raw / alpha_norm[:, None]
    search_dir = right_vector
    solution = jnp.zeros_like(right_vector)
    phi_bar = beta_norm
    rho_bar = alpha_norm
    for iteration in range(ITERS):
        forward_out = forward(right_raw.astype(jnp.bfloat16))
        left_raw = forward_out / alpha_norm[:, None] - alpha_norm[:, None] * left_vector
        backward_out = backward(left_raw.astype(jnp.bfloat16))
        beta_norm = data_norm(left_raw)
        right_raw = backward_out / beta_norm[:, None] - beta_norm[:, None] * right_vector
        alpha_next = model_norm(right_raw)
        left_vector = left_raw / beta_norm[:, None]
        right_vector = right_raw / alpha_next[:, None]
        rho_value = jnp.sqrt(rho_bar * rho_bar + beta_norm * beta_norm)
        cosine = rho_bar / rho_value
        sine_value = beta_norm / rho_value
        theta_value = sine_value * alpha_next
        rho_bar = -cosine * alpha_next
        phi_value = cosine * phi_bar
        phi_bar = sine_value * phi_bar
        solution = solution + (phi_value / rho_value)[:, None] * search_dir
        search_dir = right_vector - (theta_value / rho_value)[:, None] * search_dir
        alpha_norm = alpha_next
    fitted = forward(solution.astype(jnp.bfloat16))
    residual = begin - fitted
    return (solution.reshape(solution.shape[0], 1, -1), residual.reshape(residual.shape[0], 1, -1))


def solution(mesh):
    in_specs = (
        P(None, "col", "row"),
        P("row", "col", None, None, None),
        P("row", "col", None),
        P("row", "col", None),
        P("row", "col"),
    )
    out_specs = (P(None, "row", "col"), P(None, "col", "row"))
    return jax.shard_map(local, mesh=mesh, in_specs=in_specs, out_specs=out_specs, check_vma=False)
```

profile of v0, /device:TPU:1, one launch (start us, length us, event | category | flops | bytes accessed | tf_op | source)
XLA Modules:
  0.0 703.5 jit_solution(5239885321689624086)
XLA Ops:
  7.2 0.0 reduce-scatter.6.cloned.1.call-start
  7.2 0.8 copy.53
  8.1 44.0 %all_gather.15 = bf16[64,4096]{1,0:T(8,128)(2,1)S(1)} all-gather(bf16[64,256]{1,0:T(8,128)(2,1)S(1)} %bitcast.100), channel_id=1, replica_groups=mesh['row'=16,'col'=16] {'row'}, dimensions={1}, use_global_device_ids=true | all-gather | bytes 557056 | tf_op jit(solution)/shard_map/all_gather | solution.py:55
  52.0 0.1 copy.18
  52.8 1.4 fusion.32
  54.2 0.0 copy-start.2
  54.2 5.5 fusion.8
  59.7 0.0 copy-done.2
  59.7 4.6 fusion.18
  64.3 1.0 copy.19
  65.2 0.0 reduce-scatter.6.cloned.1.call-update
  65.3 0.0 reduce-scatter.8.cloned.1.call-start
  65.3 0.0 copy-done
  65.3 0.1 fusion.20
  65.4 81.3 %psum.35 = f32[64]{0:T(128)S(1)} all-reduce(f32[64]{0:T(128)S(1)} %fusion.20), channel_id=1, replica_groups=mesh['row'=16,'col'=16] {'row','col'}, use_global_device_ids=true, to_apply=%region_2.0 | all-reduce | flops 64 | bytes 512 | tf_op jit(solution)/shard_map/psum | solution.py:64
  146.7 0.0 reduce-scatter.6.cloned.1.call-done
  146.7 0.9 fusion.34
  147.7 20.0 %all_gather.16 = bf16[64,2048]{1,0:T(8,128)(2,1)S(1)} all-gather(bf16[64,128]{1,0:T(8,128)(2,1)S(1)} %get-tuple-element.13), channel_id=1, replica_groups=mesh['row'=16,'col'=16] {'col'}, dimensions={1}, use_global_device_ids=true | all-gather | bytes 278528 | tf_op jit(solution)/shard_map/all_gather | solution.py:49
  167.7 0.1 copy.20
  167.7 0.8 fusion.50
  168.5 0.0 copy-start.3
  168.5 5.9 fusion.6
  174.4 4.6 fusion.16
  179.1 1.6 copy.21
  180.6 0.0 reduce-scatter.8.cloned.1.call-update
  180.7 0.0 reduce-scatter.10.cloned.1.call-start
  180.7 73.6 %psum.36 = f32[64]{0:T(128)S(1)} all-reduce(f32[64]{0:T(128)S(1)} %get-tuple-element.14), channel_id=1, replica_groups=mesh['row'=16,'col'=16] {'row','col'}, use_global_device_ids=true, to_apply=%region_4.0 | all-reduce | flops 64 | bytes 512 | tf_op jit(solution)/shard_map/psum | solution.py:67
  254.3 3.8 reduce-scatter.8.cloned.1.call-done
  258.1 1.0 multiply_reduce_fusion.1
  259.2 39.3 %all_gather.17 = bf16[64,4096]{1,0:T(8,128)(2,1)S(1)} all-gather(bf16[64,256]{1,0:T(8,128)(2,1)S(1)} %convert_element_type.46), channel_id=1, replica_groups=mesh['row'=16,'col'=16] {'row'}, dimensions={1}, use_global_device_ids=true | all-gather | bytes 557056 | tf_op jit(solution)/shard_map/all_gather | solution.py:55
  298.5 0.1 copy.22
  298.6 0.8 fusion.30
  299.4 5.4 fusion.4
  304.8 4.6 fusion.14
  309.4 1.0 copy.23
  310.4 0.0 reduce-scatter.10.cloned.1.call-update
  310.4 0.0 reduce-scatter.12.cloned.1.call-start
  310.4 82.0 %psum.37 = f32[64]{0:T(128)S(1)} all-reduce(f32[64]{0:T(128)S(1)} %get-tuple-element.11), channel_id=1, replica_groups=mesh['row'=16,'col'=16] {'row','col'}, use_global_device_ids=true, to_apply=%region_7.0 | all-reduce | flops 64 | bytes 512 | tf_op jit(solution)/shard_map/psum | solution.py:64
  392.4 0.0 reduce-scatter.10.cloned.1.call-done
  392.5 0.8 fusion.77
  393.3 20.3 %all_gather.18 = bf16[64,2048]{1,0:T(8,128)(2,1)S(1)} all-gather(bf16[64,128]{1,0:T(8,128)(2,1)S(1)} %get-tuple-element.9), channel_id=1, replica_groups=mesh['row'=16,'col'=16] {'col'}, dimensions={1}, use_global_device_ids=true | all-gather | bytes 278528 | tf_op jit(solution)/shard_map/all_gather | solution.py:49
  413.6 0.1 copy.24
  413.7 0.7 fusion.48
  414.4 5.9 fusion.2
  420.3 4.6 fusion.12
  425.0 1.6 copy.25
  426.6 0.0 reduce-scatter.12.cloned.1.call-update
  426.6 0.0 reduce-scatter.14.cloned.1.call-start
  426.7 0.1 multiply_reduce_fusion.2
  426.8 73.1 %psum.38 = f32[64]{0:T(128)S(1)} all-reduce(f32[64]{0:T(128)S(1)} %multiply_reduce_fusion.2), channel_id=1, replica_groups=mesh['row'=16,'col'=16] {'row','col'}, use_global_device_ids=true, to_apply=%region_10.0 | all-reduce | flops 64 | bytes 512 | tf_op jit(solution)/shard_map/psum | solution.py:67
  499.9 6.0 reduce-scatter.12.cloned.1.call-done
  505.9 1.0 multiply_reduce_fusion
  507.0 75.6 %psum.39 = f32[64]{0:T(128)S(1)} all-reduce(f32[64]{0:T(128)S(1)} %multiply_reduce_fusion), channel_id=1, replica_groups=mesh['row'=16,'col'=16] {'row','col'}, use_global_device_ids=true, to_apply=%region_13.0 | all-reduce | flops 64 | bytes 512 | tf_op jit(solution)/shard_map/psum | solution.py:64
  582.6 0.7 fusion.74
  583.3 20.6 %all_gather.19 = bf16[64,2048]{1,0:T(8,128)(2,1)S(1)} all-gather(bf16[64,128]{1,0:T(8,128)(2,1)S(1)} %get-tuple-element.2), channel_id=1, replica_groups=mesh['row'=16,'col'=16] {'col'}, dimensions={1}, use_global_device_ids=true | all-gather | bytes 278528 | tf_op jit(solution)/shard_map/all_gather | solution.py:49
  603.9 0.1 copy.26
  604.0 0.7 fusion.46
  604.8 5.9 fusion
  610.7 4.6 fusion.10
  615.3 1.6 copy.27
  616.9 0.0 reduce-scatter.14.cloned.1.call-update
  616.9 78.3 %reduce-scatter.14.cloned.1.call-done = f32[64,256]{1,0:T(8,128)} async-done(((f32[64,4096]{1,0:T(8,128)}), f32[64,256]{1,0:T(8,128)}) %reduce-scatter.14.cloned.1.call-update) | async-done | bytes 65552 | tf_op jit(solution)/shard_map/reduce_scatter | solution.py:50
  695.2 0.8 bitcast_subtract_fusion
  696.1 0.7 reshape.65
  (12 shorter events, 0.1 us)
Async XLA Ops:
  7.2 139.5 %reduce-scatter.6.cloned.1.call-start = ((), (), s32[]{:S(2)}) async-start(), calls=%async_computation.5 | async-start | bytes 557056 | tf_op jit(solution)/shard_map/reduce_scatter | solution.py:56
  54.2 5.5 copy-start.2
  59.7 5.6 copy-start
  65.3 192.8 %reduce-scatter.8.cloned.1.call-start = ((), (), s32[]{:S(2)}) async-start(), calls=%async_computation.6 | async-start | bytes 1114112 | tf_op jit(solution)/shard_map/reduce_scatter | solution.py:50
  168.5 5.9 copy-start.3
  180.7 211.8 %reduce-scatter.10.cloned.1.call-start = ((), (), s32[]{:S(2)}) async-start(), calls=%async_computation.7 | async-start | bytes 557056 | tf_op jit(solution)/shard_map/reduce_scatter | solution.py:56
  304.8 87.7 %copy-start.1 = (f32[64,128]{1,0:T(8,128)S(1)}, f32[64,128]{1,0:T(8,128)}, u32[]{:S(2)}) copy-start(f32[64,128]{1,0:T(8,128)} %reduce-scatter.6.cloned.1.call-done) | copy-start | bytes 98308
  310.4 195.5 %reduce-scatter.12.cloned.1.call-start = ((), (), s32[]{:S(2)}) async-start(), calls=%async_computation.8 | async-start | bytes 1114112 | tf_op jit(solution)/shard_map/reduce_scatter | solution.py:50
  426.6 268.6 %reduce-scatter.14.cloned.1.call-start = ((), (), s32[]{:S(2)}) async-start(), calls=%async_computation.9 | async-start | bytes 1114112 | tf_op jit(solution)/shard_map/reduce_scatter | solution.py:50
Sparse Core Ops, SparseCore 0:
  65.4 61.5 reduce-scatter.5
  180.8 77.2 reduce-scatter.7
  310.5 64.9 reduce-scatter.9
  426.7 79.1 reduce-scatter.11
  617.0 78.1 reduce-scatter.13
where the time goes:
time: 712 us; the launch traced here: 703 us
  blocking collectives  530 us (74%)
  waiting for transfers between devices  88.2 us (12%)
  matrix products  56.1 us (8%)
  between operations  14.8 us (2%)
  local copies, waits for them, and re-layouts  8.6 us (1%)
    psum x3, blocking collectives, data_norm(): lax.psum(jnp.sum(vector * vector, axis=1), ('row', 'col')) + EPSILON  239 us
    psum x2, blocking collectives, model_norm(): lax.psum(jnp.sum(vector * vector, axis=1), ('row', 'col')) + EPSILON  147 us
    reduce_scatter x3, waiting for transfers between devices, forward(): lax.psum_scatter(forward_part(whole, tile_set, col_pick, row_add), 'row',...  88.1 us
    all_gather x2, blocking collectives, backward(): whole = lax.all_gather(vector_low, 'row', axis=1, tiled=True)  83.3 us
    all_gather x3, blocking collectives, forward(): whole = lax.all_gather(vector_low, 'col', axis=1, tiled=True)  60.9 us
    dot_general x3, matrix products, forward_part(): jnp.einsum('tij,trj->tri', tile_set, picked, preferred_element_type=jnp.f...  17.7 us
  transfers between devices with their start and end apart: 5, of which 3 were waited for; matrix products, arithmetic and copies ran while one was open for 0% of the time, Pallas kernels for 0%

commit v1 on v0

v1 whole, which is shorter than its diff:
```python
import functools

import jax
import jax.numpy as jnp
from jax import lax
from jax.experimental import pallas as pl
from jax.experimental.pallas import tpu as pltpu
from jax.sharding import PartitionSpec as P

MESH = pl.DeviceIdType.MESH
EPSILON = 1e-06
TILE = 256
PIECE = 128
NZ = 4


def order(i):
    return i + lax.div(i, 2) - 2 * lax.div(i, 3)


ORDER = {2: (0, 1), 4: (0, 1, 3, 2)}


def dot(a, b):
    return jnp.dot(a, b, preferred_element_type=jnp.float32)


def kernel(
    dims,
    rows_s,
    cols_s,
    count_s,
    rhs,
    tiles_hbm,
    sol_out,
    res_out,
    tiles,
    ttiles,
    idx_v,
    idx_s,
    zb,
    s1send,
    s1recv,
    s2send,
    s2recv,
    part,
    csend,
    crecv,
    wrecv,
    wfull,
    outp,
    first_f,
    nsend,
    nrecv,
    tile_sem,
    idx_sem,
    zb_send,
    zb_z,
    zb_x,
    s1_send,
    s1_sem,
    s2_send,
    s2_sem,
    c_send,
    c_sem,
    w_send,
    w_sem,
    n_send,
    n_sem,
):
    nz, nx, nc, cbg, tpd, sides = dims
    nr = nz * nx
    r = lax.axis_index("row")
    c = lax.axis_index("col")
    zh = lax.div(r, nx)
    x = lax.rem(r, nx)

    load = pltpu.make_async_copy(tiles_hbm.at[0, 0], tiles.at[pl.ds(0, tpd)], tile_sem)
    load.start()

    barrier = pltpu.get_barrier_semaphore()
    for d in range(1, nr):
        pl.semaphore_signal(barrier, inc=1, device_id=(lax.rem(r + d, nr), c), device_id_type=MESH)
    for d in range(1, nc):
        pl.semaphore_signal(barrier, inc=1, device_id=(r, lax.rem(c + d, nc)), device_id_type=MESH)

    def send(src, dst, send_sem, recv_sem, device):
        pltpu.make_async_remote_copy(
            src_ref=src,
            dst_ref=dst,
            send_sem=send_sem,
            recv_sem=recv_sem,
            device_id=device,
            device_id_type=MESH,
        ).start()

    def take(ref, sem):
        pltpu.make_async_copy(ref, ref, sem).wait()

    def x_peer(dx):
        return (zh * nx + lax.rem(x + dx, nx), c)

    def z_peer(dz):
        return (lax.rem(zh + dz, nz) * nx + x, c)

    eye = (
        lax.broadcasted_iota(jnp.int32, (sides, 128), 0)
        == lax.broadcasted_iota(jnp.int32, (sides, 128), 1)
    ).astype(jnp.float32)

    def to_row(column):
        return jnp.sum(column * eye, axis=0, keepdims=True)

    def to_column(row):
        return jnp.sum(row * eye, axis=1, keepdims=True)

    def square_sum(array):
        return to_row(jnp.sum(array * array, axis=1, keepdims=True))

    def norm_start(n, value, axis):
        nsend[n] = jnp.broadcast_to(value, (8, 128))
        for d in range(1, nr if axis == "row" else nc):
            device = (lax.rem(r + d, nr), c) if axis == "row" else (r, lax.rem(c + d, nc))
            send(nsend.at[n], nrecv.at[n, d], n_send.at[n], n_sem.at[n], device)

    def norm_finish(n, value, axis):
        size = nr if axis == "row" else nc
        take(nrecv.at[n, pl.ds(1, size - 1)], n_sem.at[n])
        for d in range(1, size):
            value = value + nrecv[n, d, 0:1, :]
        return value

    def make_index():
        lane = lax.broadcasted_iota(jnp.int32, (8, 128), 1)
        count = count_s[0, 0]

        def one(t, table):
            key = rows_s[0, 0, t] * cbg + cols_s[0, 0, t]
            key = jnp.where(t < count, key, -1)
            return jnp.where(lane == key, t, table)

        idx_v[...] = lax.fori_loop(0, tpd, one, jnp.full((8, 128), tpd, jnp.int32))
        copy = pltpu.make_async_copy(idx_v, idx_s, idx_sem)
        copy.start()
        copy.wait()

    def make_transposed():
        load.wait()
        tiles[tpd] = jnp.zeros((TILE, TILE), jnp.bfloat16)
        ttiles[tpd] = jnp.zeros((TILE, TILE), jnp.bfloat16)

        def some(step, carry):
            for u in range(4):
                ttiles[step * 4 + u] = tiles[step * 4 + u].T
            return carry

        lax.fori_loop(0, tpd // 4, some, 0)

    def backward(inst, vector, n, first):
        zb[inst, 0] = vector.astype(jnp.bfloat16)
        if first:
            pl.semaphore_wait(barrier, nr + nc - 2)
        for dz in reversed(ORDER[nz][1:]):
            send(zb.at[inst, 0], zb.at[inst, dz * nx], zb_send.at[inst], zb_z.at[inst, dz], z_peer(dz))
        for dx in reversed(ORDER[nx][1:]):
            send(zb.at[inst, 0], zb.at[inst, dx], zb_send.at[inst], zb_x.at[inst, 0], x_peer(dx))
        squares = square_sum(vector)
        norm_start(n, squares, "row")
        if first:
            make_index()
        for dz in ORDER[nz][1:]:
            take(zb.at[inst, dz * nx], zb_z.at[inst, dz])
            for dx in reversed(ORDER[nx][1:]):
                send(
                    zb.at[inst, dz * nx],
                    zb.at[inst, dz * nx + dx],
                    zb_send.at[inst],
                    zb_x.at[inst, dz],
                    x_peer(dx),
                )
        if first:
            make_transposed()
        for piece in range(nc):
            outp[piece] = jnp.zeros((sides, PIECE), jnp.float32)

        def group(i, carry):
            dz = order(i)
            take(zb.at[inst, pl.ds(dz * nx + 1, nx - 1)], zb_x.at[inst, dz])
            origin = lax.rem(zh - dz + nz, nz) * nx
            for k in range(cbg):
                total = None
                for dx in range(nx):
                    block = origin + lax.rem(x - dx + nx, nx)
                    product = dot(zb[inst, dz * nx + dx], tiles[idx_s[0, block * cbg + k]])
                    total = product if total is None else total + product
                outp[2 * k] += total[:, :PIECE]
                outp[2 * k + 1] += total[:, PIECE:]
            return carry

        lax.fori_loop(0, nz, group, 0)
        squares = norm_finish(n, squares, "row")
        norm_start(n + 1, squares, "col")
        for d in range(1, nc):
            peer = lax.rem(c + d, nc)
            csend[inst, d] = outp[peer].astype(jnp.bfloat16)
            send(csend.at[inst, d], crecv.at[inst, d], c_send.at[inst], c_sem.at[inst], (r, peer))
        total = outp[c]
        take(crecv.at[inst, pl.ds(1, nc - 1)], c_sem.at[inst])
        for d in range(1, nc):
            total = total + crecv[inst, d].astype(jnp.float32)
        squares = norm_finish(n + 1, squares, "col")
        return total, jnp.sqrt(to_column(squares) + EPSILON)

    def forward(inst, vector, n):
        wrecv[inst, 0] = vector.astype(jnp.bfloat16)
        for d in range(1, nc):
            send(
                wrecv.at[inst, 0],
                wrecv.at[inst, d],
                w_send.at[inst],
                w_sem.at[inst],
                (r, lax.rem(c + d, nc)),
            )
        squares = square_sum(vector)
        norm_start(n, squares, "col")
        take(wrecv.at[inst, pl.ds(1, nc - 1)], w_sem.at[inst])
        for k in range(cbg):
            wfull[k, :, :PIECE] = wrecv[inst, lax.rem(c - 2 * k + nc, nc)]
            wfull[k, :, PIECE:] = wrecv[inst, lax.rem(c - 2 * k - 1 + nc, nc)]

        def group(i, carry):
            dz = order(nz - 1 - i)
            for dx in reversed(ORDER[nx]):
                block = lax.rem(zh + dz, nz) * nx + lax.rem(x + dx, nx)
                total = None
                for k in range(cbg):
                    product = dot(wfull[k], ttiles[idx_s[0, block * cbg + k]])
                    total = product if total is None else total + product
                if dx == 0:
                    part[dz] = total
                else:
                    slot = dz * nx + dx
                    s1send[inst, slot] = total.astype(jnp.bfloat16)
                    send(
                        s1send.at[inst, slot],
                        s1recv.at[inst, slot],
                        s1_send.at[inst],
                        s1_sem.at[inst, dz],
                        x_peer(dx),
                    )
            return carry

        lax.fori_loop(0, nz, group, 0)
        squares = norm_finish(n, squares, "col")
        norm_start(n + 1, squares, "row")
        total = None
        for dz in reversed(ORDER[nz]):
            take(s1recv.at[inst, pl.ds(dz * nx + 1, nx - 1)], s1_sem.at[inst, dz])
            total = part[dz]
            for dx in range(1, nx):
                total = total + s1recv[inst, dz * nx + dx].astype(jnp.float32)
            if dz:
                s2send[inst, dz] = total.astype(jnp.bfloat16)
                send(
                    s2send.at[inst, dz],
                    s2recv.at[inst, dz],
                    s2_send.at[inst],
                    s2_sem.at[inst],
                    z_peer(dz),
                )
        take(s2recv.at[inst, pl.ds(1, nz - 1)], s2_sem.at[inst])
        for dz in range(1, nz):
            total = total + s2recv[inst, dz].astype(jnp.float32)
        squares = norm_finish(n + 1, squares, "row")
        return total, jnp.sqrt(to_column(squares) + EPSILON)

    begin = rhs[...]
    back, beta0 = backward(0, begin, 0, True)
    right_raw = back / beta0
    forward1, alpha0 = forward(0, right_raw, 2)
    first_f[...] = forward1
    right0 = right_raw / alpha0
    left_raw = forward1 / alpha0 - alpha0 * (begin / beta0)
    back, beta1 = backward(1, left_raw, 4, False)
    right_raw = back / beta1 - beta1 * right0
    forward2, alpha1 = forward(1, right_raw, 6)
    right1 = right_raw / alpha1
    left_raw = forward2 / alpha1 - alpha1 * (left_raw / beta1)

    squares = square_sum(left_raw)
    norm_start(8, squares, "row")
    rho_bar = alpha0
    phi_bar = beta0
    rho_value = jnp.sqrt(rho_bar * rho_bar + beta1 * beta1)
    cosine = rho_bar / rho_value
    sine_value = beta1 / rho_value
    theta_value = sine_value * alpha1
    step0 = cosine * phi_bar / rho_value
    turn0 = theta_value / rho_value
    rho_bar = -cosine * alpha1
    phi_bar = sine_value * phi_bar
    squares = norm_finish(8, squares, "row")
    norm_start(9, squares, "col")
    squares = norm_finish(9, squares, "col")
    beta2 = jnp.sqrt(to_column(squares) + EPSILON)
    rho_value = jnp.sqrt(rho_bar * rho_bar + beta2 * beta2)
    step1 = rho_bar / rho_value * phi_bar / rho_value
    weight0 = step0 - step1 * turn0
    sol_out[...] = weight0 * right0 + step1 * right1
    res_out[...] = begin - (weight0 / alpha0) * first_f[...] - (step1 / alpha1) * forward2

    for inst in range(2):
        take(zb.at[inst, pl.ds(1, nr - 1)], zb_send.at[inst])
        take(s1recv.at[inst, pl.ds(0, nz * (nx - 1))], s1_send.at[inst])
        take(s2recv.at[inst, pl.ds(1, nz - 1)], s2_send.at[inst])
        take(crecv.at[inst, pl.ds(1, nc - 1)], c_send.at[inst])
        take(wrecv.at[inst, pl.ds(1, nc - 1)], w_send.at[inst])
    for n in range(10):
        size = nr if n in (0, 3, 4, 7, 8) else nc
        take(nrecv.at[n, pl.ds(1, size - 1)], n_send.at[n])


def local(dims, right_side, tile_values, tile_rows, tile_cols, tile_count):
    nz, nx, nc, cbg, tpd, sides = dims
    nr = nz * nx
    bf16, f32, i32 = jnp.bfloat16, jnp.float32, jnp.int32
    smem = pl.BlockSpec(memory_space=pltpu.SMEM)
    vmem = pl.BlockSpec(memory_space=pltpu.VMEM)
    dma = pltpu.SemaphoreType.DMA
    solution, residual = pl.pallas_call(
        functools.partial(kernel, dims),
        out_shape=(
            jax.ShapeDtypeStruct((sides, PIECE), f32),
            jax.ShapeDtypeStruct((sides, TILE), f32),
        ),
        in_specs=[smem, smem, smem, vmem, pl.BlockSpec(memory_space=pl.ANY)],
        out_specs=(vmem, vmem),
        scratch_shapes=[
            pltpu.VMEM((tpd + 1, TILE, TILE), bf16),
            pltpu.VMEM((tpd + 1, TILE, TILE), bf16),
            pltpu.VMEM((8, 128), i32),
            pltpu.SMEM((8, 128), i32),
            pltpu.VMEM((2, nr, sides, TILE), bf16),
            pltpu.VMEM((2, nr, sides, TILE), bf16),
            pltpu.VMEM((2, nr, sides, TILE), bf16),
            pltpu.VMEM((2, nz, sides, TILE), bf16),
            pltpu.VMEM((2, nz, sides, TILE), bf16),
            pltpu.VMEM((nz, sides, TILE), f32),
            pltpu.VMEM((2, nc, sides, PIECE), bf16),
            pltpu.VMEM((2, nc, sides, PIECE), bf16),
            pltpu.VMEM((2, nc, sides, PIECE), bf16),
            pltpu.VMEM((cbg, sides, TILE), bf16),
            pltpu.VMEM((nc, sides, PIECE), f32),
            pltpu.VMEM((sides, TILE), f32),
            pltpu.VMEM((10, 8, 128), f32),
            pltpu.VMEM((10, max(nr, nc), 8, 128), f32),
            dma,
            dma,
            dma((2,)),
            dma((2, nz)),
            dma((2, nz)),
            dma((2,)),
            dma((2, nz)),
            dma((2,)),
            dma((2,)),
            dma((2,)),
            dma((2,)),
            dma((2,)),
            dma((2,)),
            dma((10,)),
            dma((10,)),
        ],
        compiler_params=pltpu.CompilerParams(
            collective_id=0, has_side_effects=True, vmem_limit_bytes=48 * 2**20
        ),
        name="lsqr",
    )(tile_rows, tile_cols, tile_count, right_side[:, 0, :], tile_values)
    return solution.reshape(sides, 1, PIECE), residual.reshape(sides, 1, TILE)


def solution(mesh):
    in_specs = (
        P(None, "col", "row"),
        P("row", "col", None, None, None),
        P("row", "col", None),
        P("row", "col", None),
        P("row", "col"),
    )
    out_specs = (P(None, "row", "col"), P(None, "col", "row"))
    nr, nc = mesh.shape["row"], mesh.shape["col"]
    nz = 4 if nr == 16 else 2

    def program(right_side, tile_values, tile_rows, tile_cols, tile_count):
        dims = (nz, nr // nz, nc, nc * PIECE // TILE, tile_values.shape[2], right_side.shape[0])
        return jax.shard_map(
            functools.partial(local, dims),
            mesh=mesh,
            in_specs=in_specs,
            out_specs=out_specs,
            check_vma=False,
        )(right_side, tile_values, tile_rows, tile_cols, tile_count)

    return program
```

time: 712 us -> 105 us (0.15); the launches traced: 703 us -> 105 us
  blocking collectives: 530 us -> 0 us
  Pallas kernels: 0 us -> 99.8 us
  waiting for transfers between devices: 88.2 us -> 0 us
  matrix products: 56.1 us -> 0 us
  between operations: 14.8 us -> 1.29 us
    psum x5 -> x0, blocking collectives: 386 us -> none  [the longest x3 239 us: data_norm(): lax.psum(jnp.sum(vector * vector, axis=1), ('row', 'col')) + EPSILON]
    all_gather x5 -> x0, blocking collectives: 144 us -> none  [the longest x2 83.3 us: backward(): whole = lax.all_gather(vector_low, 'row', axis=1, tiled=True)]
    pallas_call x0 -> x1, Pallas kernels: none -> 99.8 us  [local(): pl.pallas_call(functools.partial(kernel, dims), out_shape=(jax.ShapeDtype...]
    reduce_scatter x5 -> x0, waiting for transfers between devices: 88.1 us -> none  [the longest x3 88.1 us: forward(): lax.psum_scatter(forward_part(whole, tile_set, col_pick, row_add), 'row',...]
    dot_general x15 -> x0, matrix products: 56.1 us -> none  [the longest x3 17.7 us: forward_part(): jnp.einsum('tij,trj->tri', tile_set, picked, preferred_element_type=jnp.f...]
  transfers between devices with their start and end apart: 5 -> 0, of which waited for: 3 -> 0; matrix products, arithmetic and copies ran while one was open for 0% -> 0% of each run, Pallas kernels for 0% -> 0%
where the time goes in v1:
time: 105 us
  Pallas kernels  99.8 us (95%)
  local copies, waits for them, and re-layouts  3.47 us (3%)
  between operations  1.29 us (1%)
    pallas_call x1, Pallas kernels, local(): pl.pallas_call(functools.partial(kernel, dims), out_shape=(jax.ShapeDtype...  99.8 us
    unnamed x7, local copies, waits for them, and re-layouts  3.47 us

profile of v1, /device:TPU:1, one launch (start us, length us, event | category | flops | bytes accessed | tf_op | source)
XLA Modules:
  0.0 104.5 jit_solution(13729021116621531938)
XLA Ops:
  1.3 0.8 copy.11
  2.1 0.0 copy-start
  2.1 0.7 copy-done
  2.8 0.0 copy-start.1
  2.8 0.7 copy-done.1
  3.4 99.8 %lsqr.1 = (f32[64,128]{1,0:T(8,128)S(1)}, f32[64,256]{1,0:T(8,128)S(1)}) custom-call(s32[1,1,64]{2,1,0:T(1,128)S(1)} %copy-done, s32[1,1,64]{2,1,0:T(1,128)S(1)} %copy-done.1, s32[1,1]{1,0:T(1,128)S(6)} %copy.13.count_s, f32[64,256]{1,0:T(8,128)S(1)} %bitcast.7, bf16[1,1,64,256,256]{4,3,2,1,0:T(8,128)(2,1)} %tiles_hbm.1), custom_call_target="tpu_custom_call" | custom-call | tf_op jit(solution)/shard_map/lsqr/pallas_call | solution.py:330
  103.2 0.7 copy.8
  103.9 0.6 copy.14
Async XLA Ops:
  2.1 0.7 copy-start
  2.8 0.7 copy-start.1

commit v2 on v1

--- a/solution.py
+++ b/solution.py
@@ -1,4 +1,5 @@
 import functools
+import itertools
 
 import jax
 import jax.numpy as jnp
@@ -27,13 +28,17 @@
 
 def kernel(
     dims,
+    rows_hbm,
+    cols_hbm,
+    count_hbm,
+    rhs_hbm,
+    tiles_hbm,
+    sol_out,
+    res_out,
     rows_s,
     cols_s,
     count_s,
     rhs,
-    tiles_hbm,
-    sol_out,
-    res_out,
     tiles,
     ttiles,
     idx_v,
@@ -52,7 +57,10 @@
     first_f,
     nsend,
     nrecv,
+    frecv,
     tile_sem,
+    small_sem,
+    rhs_sem,
     idx_sem,
     zb_send,
     zb_z,
@@ -70,6 +78,7 @@
 ):
     nz, nx, nc, cbg, tpd, sides = dims
     nr = nz * nx
+    ny = nc // 4
     r = lax.axis_index("row")
     c = lax.axis_index("col")
     zh = lax.div(r, nx)
@@ -77,12 +86,48 @@
 
     load = pltpu.make_async_copy(tiles_hbm.at[0, 0], tiles.at[pl.ds(0, tpd)], tile_sem)
     load.start()
+    small = [
+        pltpu.make_async_copy(rows_hbm, rows_s, small_sem.at[0]),
+        pltpu.make_async_copy(cols_hbm, cols_s, small_sem.at[1]),
+        pltpu.make_async_copy(count_hbm, count_s, small_sem.at[2]),
+        pltpu.make_async_copy(rhs_hbm.at[:, 0, :], rhs, rhs_sem),
+    ]
+    for copy in small:
+        copy.start()
 
     barrier = pltpu.get_barrier_semaphore()
-    for d in range(1, nr):
-        pl.semaphore_signal(barrier, inc=1, device_id=(lax.rem(r + d, nr), c), device_id_type=MESH)
-    for d in range(1, nc):
-        pl.semaphore_signal(barrier, inc=1, device_id=(r, lax.rem(c + d, nc)), device_id_type=MESH)
+
+    def x_peer(dx):
+        return (zh * nx + lax.rem(x + dx, nx), c)
+
+    def z_peer(dz):
+        return (lax.rem(zh + dz, nz) * nx + x, c)
+
+    def at_offset(offset, dc):
+        z = lax.rem(2 * zh + lax.rem(lax.div(c, 2), 2) + offset[0], 2 * nz)
+        y = lax.rem(lax.div(c, 4) + offset[2], ny)
+        core = lax.rem(lax.rem(c, 2) + dc, 2)
+        return (
+            lax.div(z, 2) * nx + lax.rem(x + offset[1], nx),
+            y * 4 + lax.rem(z, 2) * 2 + core,
+        )
+
+    sizes = (2 * nz, nx, ny)
+    offsets = sorted(
+        itertools.product(*map(range, sizes)),
+        key=lambda o: -sum(min(d, s - d) for d, s in zip(o, sizes)),
+    )
+    peers = {
+        "x": [x_peer(dx) for dx in range(1, nx)],
+        "z": [z_peer(dz) for dz in range(1, nz)],
+        "row": [(lax.rem(r + d, nr), c) for d in range(1, nr)],
+        "col": [(r, lax.rem(c + d, nc)) for d in range(1, nc)],
+        "core": [at_offset((0, 0, 0), 1)],
+        "chips": [at_offset(o, 0) for o in offsets if any(o)],
+    }
+    greeted = peers["z"] + peers["x"] + peers["col"]
+    for device in greeted:
+        pl.semaphore_signal(barrier, inc=1, device_id=device, device_id_type=MESH)
 
     def send(src, dst, send_sem, recv_sem, device):
         pltpu.make_async_remote_copy(
@@ -97,12 +142,6 @@
     def take(ref, sem):
         pltpu.make_async_copy(ref, ref, sem).wait()
 
-    def x_peer(dx):
-        return (zh * nx + lax.rem(x + dx, nx), c)
-
-    def z_peer(dz):
-        return (lax.rem(zh + dz, nz) * nx + x, c)
-
     eye = (
         lax.broadcasted_iota(jnp.int32, (sides, 128), 0)
         == lax.broadcasted_iota(jnp.int32, (sides, 128), 1)
@@ -117,18 +156,17 @@
     def square_sum(array):
         return to_row(jnp.sum(array * array, axis=1, keepdims=True))
 
-    def norm_start(n, value, axis):
-        nsend[n] = jnp.broadcast_to(value, (8, 128))
-        for d in range(1, nr if axis == "row" else nc):
-            device = (lax.rem(r + d, nr), c) if axis == "row" else (r, lax.rem(c + d, nc))
-            send(nsend.at[n], nrecv.at[n, d], n_send.at[n], n_sem.at[n], device)
-
-    def norm_finish(n, value, axis):
-        size = nr if axis == "row" else nc
-        take(nrecv.at[n, pl.ds(1, size - 1)], n_sem.at[n])
-        for d in range(1, size):
-            value = value + nrecv[n, d, 0:1, :]
-        return value
+    def norm_start(n, value, kind):
+        nsend[pl.ds(n, 1), :] = value
+        slots = frecv if kind == "chips" else nrecv.at[n]
+        for d, device in enumerate(peers[kind]):
+            send(nsend.at[pl.ds(n, 1)], slots.at[pl.ds(d, 1)], n_send.at[n], n_sem.at[n], device)
+
+    def norm_finish(n, value, kind):
+        slots = frecv if kind == "chips" else nrecv.at[n]
+        size = len(peers[kind])
+        take(slots.at[pl.ds(0, size)], n_sem.at[n])
+        return value + jnp.sum(slots[0:size, :], axis=0, keepdims=True)
 
     def make_index():
         lane = lax.broadcasted_iota(jnp.int32, (8, 128), 1)
@@ -144,28 +182,34 @@
         copy.start()
         copy.wait()
 
-    def make_transposed():
-        load.wait()
-        tiles[tpd] = jnp.zeros((TILE, TILE), jnp.bfloat16)
-        ttiles[tpd] = jnp.zeros((TILE, TILE), jnp.bfloat16)
-
+    def make_transposed(begin, end):
         def some(step, carry):
             for u in range(4):
                 ttiles[step * 4 + u] = tiles[step * 4 + u].T
             return carry
 
-        lax.fori_loop(0, tpd // 4, some, 0)
-
-    def backward(inst, vector, n, first):
+        lax.fori_loop(begin // 4, end // 4, some, 0)
+
+    def backward(inst, vector, prepare, first):
         zb[inst, 0] = vector.astype(jnp.bfloat16)
+        squares = square_sum(vector) if first else None
         if first:
-            pl.semaphore_wait(barrier, nr + nc - 2)
+            tiles[tpd] = jnp.zeros((TILE, TILE), jnp.bfloat16)
+            ttiles[tpd] = jnp.zeros((TILE, TILE), jnp.bfloat16)
+            load.wait()
+            make_transposed(0, tpd // 2)
+            pl.semaphore_wait(barrier, len(greeted))
         for dz in reversed(ORDER[nz][1:]):
             send(zb.at[inst, 0], zb.at[inst, dz * nx], zb_send.at[inst], zb_z.at[inst, dz], z_peer(dz))
         for dx in reversed(ORDER[nx][1:]):
             send(zb.at[inst, 0], zb.at[inst, dx], zb_send.at[inst], zb_x.at[inst, 0], x_peer(dx))
-        squares = square_sum(vector)
-        norm_start(n, squares, "row")
+        if first:
+            norm_start(0, squares, "z")
+        else:
+            squares = square_sum(vector)
+            norm_start(3, squares, "row")
+        for piece in range(nc):
+            outp[piece] = jnp.zeros((sides, PIECE), jnp.float32)
         if first:
             make_index()
         for dz in ORDER[nz][1:]:
@@ -179,9 +223,9 @@
                     x_peer(dx),
                 )
         if first:
-            make_transposed()
-        for piece in range(nc):
-            outp[piece] = jnp.zeros((sides, PIECE), jnp.float32)
+            squares = norm_finish(0, squares, "z")
+            norm_start(1, squares, "x")
+            make_transposed(tpd // 2, tpd)
 
         def group(i, carry):
             dz = order(i)
@@ -197,23 +241,27 @@
                 outp[2 * k + 1] += total[:, PIECE:]
             return carry
 
-        lax.fori_loop(0, nz, group, 0)
-        squares = norm_finish(n, squares, "row")
-        norm_start(n + 1, squares, "col")
-        for d in range(1, nc):
+        lax.fori_loop(0, nz - 1, group, 0)
+        squares = norm_finish(1, squares, "x") if first else norm_finish(3, squares, "row")
+        n = 2 if first else 4
+        norm_start(n, squares, "col")
+        group(nz - 1, 0)
+        for d in sorted(range(1, nc), key=lambda d: -min(d, nc - d)):
             peer = lax.rem(c + d, nc)
             csend[inst, d] = outp[peer].astype(jnp.bfloat16)
             send(csend.at[inst, d], crecv.at[inst, d], c_send.at[inst], c_sem.at[inst], (r, peer))
+        squares = norm_finish(n, squares, "col")
+        norm = jnp.sqrt(to_column(squares) + EPSILON)
+        prepared = prepare(norm)
+        take(crecv.at[inst, pl.ds(1, nc - 1)], c_sem.at[inst])
         total = outp[c]
-        take(crecv.at[inst, pl.ds(1, nc - 1)], c_sem.at[inst])
         for d in range(1, nc):
             total = total + crecv[inst, d].astype(jnp.float32)
-        squares = norm_finish(n + 1, squares, "col")
-        return total, jnp.sqrt(to_column(squares) + EPSILON)
-
-    def forward(inst, vector, n):
+        return total, norm, prepared
+
+    def forward(inst, vector, n, prepare):
         wrecv[inst, 0] = vector.astype(jnp.bfloat16)
-        for d in range(1, nc):
+        for d in sorted(range(1, nc), key=lambda d: -min(d, nc - d)):
             send(
                 wrecv.at[inst, 0],
                 wrecv.at[inst, d],
@@ -250,9 +298,10 @@
                     )
             return carry
 
-        lax.fori_loop(0, nz, group, 0)
+        group(0, 0)
         squares = norm_finish(n, squares, "col")
         norm_start(n + 1, squares, "row")
+        lax.fori_loop(1, nz, group, 0)
         total = None
         for dz in reversed(ORDER[nz]):
             take(s1recv.at[inst, pl.ds(dz * nx + 1, nx - 1)], s1_sem.at[inst, dz])
@@ -268,27 +317,36 @@
                     s2_sem.at[inst],
                     z_peer(dz),
                 )
+        squares = norm_finish(n + 1, squares, "row")
+        norm = jnp.sqrt(to_column(squares) + EPSILON)
+        prepared = prepare(norm)
         take(s2recv.at[inst, pl.ds(1, nz - 1)], s2_sem.at[inst])
         for dz in range(1, nz):
             total = total + s2recv[inst, dz].astype(jnp.float32)
-        squares = norm_finish(n + 1, squares, "row")
-        return total, jnp.sqrt(to_column(squares) + EPSILON)
-
-    begin = rhs[...]
-    back, beta0 = backward(0, begin, 0, True)
-    right_raw = back / beta0
-    forward1, alpha0 = forward(0, right_raw, 2)
+        return total, norm, prepared
+
+    for copy in small:
+        copy.wait()
+    back, beta0, scale = backward(0, rhs[...], lambda norm: 1.0 / norm, True)
+    right_raw0 = back * scale
+    forward1, alpha0, (scale, shift) = forward(
+        0, right_raw0, 5, lambda norm: (1.0 / norm, (norm / beta0) * rhs[...])
+    )
+    left_raw1 = forward1 * scale - shift
     first_f[...] = forward1
-    right0 = right_raw / alpha0
-    left_raw = forward1 / alpha0 - alpha0 * (begin / beta0)
-    back, beta1 = backward(1, left_raw, 4, False)
-    right_raw = back / beta1 - beta1 * right0
-    forward2, alpha1 = forward(1, right_raw, 6)
-    right1 = right_raw / alpha1
-    left_raw = forward2 / alpha1 - alpha1 * (left_raw / beta1)
-
-    squares = square_sum(left_raw)
-    norm_start(8, squares, "row")
+    back, beta1, (scale, shift) = backward(
+        1, left_raw1, lambda norm: (1.0 / norm, (norm / alpha0) * right_raw0), False
+    )
+    right_raw1 = back * scale - shift
+    forward2, alpha1, (scale, shift) = forward(
+        1, right_raw1, 7, lambda norm: (1.0 / norm, (norm / beta1) * left_raw1)
+    )
+    left_raw2 = forward2 * scale - shift
+
+    squares = square_sum(left_raw2)
+    norm_start(9, squares, "core")
+    squares = norm_finish(9, squares, "core")
+    norm_start(10, squares, "chips")
     rho_bar = alpha0
     phi_bar = beta0
     rho_value = jnp.sqrt(rho_bar * rho_bar + beta1 * beta1)
@@ -299,15 +357,15 @@
     turn0 = theta_value / rho_value
     rho_bar = -cosine * alpha1
     phi_bar = sine_value * phi_bar
-    squares = norm_finish(8, squares, "row")
-    norm_start(9, squares, "col")
-    squares = norm_finish(9, squares, "col")
+    squares = norm_finish(10, squares, "chips")
     beta2 = jnp.sqrt(to_column(squares) + EPSILON)
     rho_value = jnp.sqrt(rho_bar * rho_bar + beta2 * beta2)
     step1 = rho_bar / rho_value * phi_bar / rho_value
     weight0 = step0 - step1 * turn0
-    sol_out[...] = weight0 * right0 + step1 * right1
-    res_out[...] = begin - (weight0 / alpha0) * first_f[...] - (step1 / alpha1) * forward2
+    weight0 = weight0 / alpha0
+    weight1 = step1 / alpha1
+    sol_out[...] = weight0 * right_raw0 + weight1 * right_raw1
+    res_out[...] = rhs[...] - weight0 * first_f[...] - weight1 * forward2
 
     for inst in range(2):
         take(zb.at[inst, pl.ds(1, nr - 1)], zb_send.at[inst])
@@ -315,16 +373,21 @@
         take(s2recv.at[inst, pl.ds(1, nz - 1)], s2_send.at[inst])
         take(crecv.at[inst, pl.ds(1, nc - 1)], c_send.at[inst])
         take(wrecv.at[inst, pl.ds(1, nc - 1)], w_send.at[inst])
-    for n in range(10):
-        size = nr if n in (0, 3, 4, 7, 8) else nc
-        take(nrecv.at[n, pl.ds(1, size - 1)], n_send.at[n])
+    kinds = ("z", "x", "col", "row", "col", "col", "row", "col", "row", "core")
+    for n, kind in enumerate(kinds):
+        take(nrecv.at[n, pl.ds(0, len(peers[kind]))], n_send.at[n])
+    take(frecv.at[pl.ds(0, len(peers["chips"]))], n_send.at[10])
+
+
+def place(solution, residual, sol_out, res_out):
+    sol_out[:, 0, :] = solution[...]
+    res_out[:, 0, :] = residual[...]
 
 
 def local(dims, right_side, tile_values, tile_rows, tile_cols, tile_count):
     nz, nx, nc, cbg, tpd, sides = dims
     nr = nz * nx
     bf16, f32, i32 = jnp.bfloat16, jnp.float32, jnp.int32
-    smem = pl.BlockSpec(memory_space=pltpu.SMEM)
     vmem = pl.BlockSpec(memory_space=pltpu.VMEM)
     dma = pltpu.SemaphoreType.DMA
     solution, residual = pl.pallas_call(
@@ -333,9 +396,13 @@
             jax.ShapeDtypeStruct((sides, PIECE), f32),
             jax.ShapeDtypeStruct((sides, TILE), f32),
         ),
-        in_specs=[smem, smem, smem, vmem, pl.BlockSpec(memory_space=pl.ANY)],
+        in_specs=[pl.BlockSpec(memory_space=pltpu.HBM)] * 5,
         out_specs=(vmem, vmem),
         scratch_shapes=[
+            pltpu.SMEM((1, 1, tpd), i32),
+            pltpu.SMEM((1, 1, tpd), i32),
+            pltpu.SMEM((1, 1), i32),
+            pltpu.VMEM((sides, TILE), f32),
             pltpu.VMEM((tpd + 1, TILE, TILE), bf16),
             pltpu.VMEM((tpd + 1, TILE, TILE), bf16),
             pltpu.VMEM((8, 128), i32),
@@ -352,8 +419,11 @@
             pltpu.VMEM((cbg, sides, TILE), bf16),
             pltpu.VMEM((nc, sides, PIECE), f32),
             pltpu.VMEM((sides, TILE), f32),
-            pltpu.VMEM((10, 8, 128), f32),
-            pltpu.VMEM((10, max(nr, nc), 8, 128), f32),
+            pltpu.VMEM((16, 128), f32),
+            pltpu.VMEM((10, max(nr, nc), 128), f32),
+            pltpu.VMEM((nr * nc // 2, 128), f32),
+            dma,
+            dma((3,)),
             dma,
             dma,
             dma((2,)),
@@ -367,15 +437,24 @@
             dma((2,)),
             dma((2,)),
             dma((2,)),
-            dma((10,)),
-            dma((10,)),
+            dma((11,)),
+            dma((11,)),
         ],
         compiler_params=pltpu.CompilerParams(
-            collective_id=0, has_side_effects=True, vmem_limit_bytes=48 * 2**20
+            collective_id=0, has_side_effects=True, vmem_limit_bytes=62 * 2**20
         ),
         name="lsqr",
-    )(tile_rows, tile_cols, tile_count, right_side[:, 0, :], tile_values)
-    return solution.reshape(sides, 1, PIECE), residual.reshape(sides, 1, TILE)
+    )(tile_rows, tile_cols, tile_count, right_side, tile_values)
+    return pl.pallas_call(
+        place,
+        out_shape=(
+            jax.ShapeDtypeStruct((sides, 1, PIECE), f32),
+            jax.ShapeDtypeStruct((sides, 1, TILE), f32),
+        ),
+        in_specs=[vmem, vmem],
+        out_specs=(vmem, vmem),
+        name="place",
+    )(solution, residual)
 
 
 def solution(mesh):

time: 105 us -> 93.8 us (0.89)
  Pallas kernels: 99.8 us -> 92.3 us
  local copies, waits for them, and re-layouts: 3.47 us -> 0 us
    pallas_call x1, Pallas kernels: 99.8 us -> 90.8 us  [local(): pl.pallas_call(functools.partial(kernel, dims), out_shape=(jax.ShapeDtype...]
    unnamed x7 -> x0, local copies, waits for them, and re-layouts: 3.47 us -> none
    pallas_call x0 -> x1, Pallas kernels: none -> 1.53 us  [local(): pl.pallas_call(place, out_shape=(jax.ShapeDtypeStruct((sides, 1, PIECE),...]
where the time goes in v2:
time: 93.8 us; the launch traced here: 93.6 us
  Pallas kernels  92.3 us (98%)
  between operations  1.29 us (1%)
    pallas_call x1, Pallas kernels, local(): pl.pallas_call(functools.partial(kernel, dims), out_shape=(jax.ShapeDtype...  90.8 us

profile of v2, /device:TPU:1, one launch (start us, length us, event | category | flops | bytes accessed | tf_op | source)
XLA Modules:
  0.0 93.6 jit_solution(2372540006083189200)
XLA Ops:
  1.3 90.8 %lsqr.1 = (f32[64,128]{1,0:T(8,128)}, f32[64,256]{1,0:T(8,128)}) custom-call(s32[1,1,64]{2,1,0:T(1,128)} %rows_hbm.1, s32[1,1,64]{2,1,0:T(1,128)} %cols_hbm.1, s32[1,1]{1,0:T(1,128)S(6)} %copy.7.count_hbm, f32[64,1,256]{2,1,0:T(1,128)} %rhs_hbm.1, bf16[1,1,64,256,256]{4,3,2,1,0:T(8,128)(2,1)} %tiles_hbm.1), custom_call_target="tpu_custom_call" | custom-call | tf_op jit(solution)/shard_map/lsqr/pallas_call | solution.py:393
  92.1 1.5 %place.1 = (f32[64,1,128]{2,1,0:T(1,128)}, f32[64,1,256]{2,1,0:T(1,128)}) custom-call(f32[64,128]{1,0:T(8,128)} %get-tuple-element.4.solution, f32[64,256]{1,0:T(8,128)} %get-tuple-element.5.residual), custom_call_target="tpu_custom_call" | custom-call | tf_op jit(solution)/shard_map/place/pallas_call | solution.py:448

commit v3 on v2

--- a/solution.py
+++ b/solution.py
@@ -12,7 +12,8 @@
 EPSILON = 1e-06
 TILE = 256
 PIECE = 128
-NZ = 4
+BACK_BATCH = 2
+FORWARD_BATCH = 2
 
 
 def order(i):
@@ -20,6 +21,10 @@
 
 
 ORDER = {2: (0, 1), 4: (0, 1, 3, 2)}
+
+
+def batches(items, size):
+    return [items[i : i + size] for i in range(0, len(items), size)]
 
 
 def dot(a, b):
@@ -190,14 +195,24 @@
 
         lax.fori_loop(begin // 4, end // 4, some, 0)
 
+    chips = sorted(
+        itertools.product(range(ny), range(2)), key=lambda o: (min(o[0], ny - o[0]), o[1])
+    )
+    core = lax.rem(c, 2)
+
+    def chip_at(offset, sign):
+        y = lax.rem(lax.div(c, 4) + sign * offset[0] + ny, ny)
+        return y * 2 + lax.rem(lax.rem(lax.div(c, 2), 2) + offset[1], 2)
+
+    def slot_of(offset):
+        return (offset[0] * 2 + offset[1]) * 2
+
     def backward(inst, vector, prepare, first):
         zb[inst, 0] = vector.astype(jnp.bfloat16)
         squares = square_sum(vector) if first else None
         if first:
             tiles[tpd] = jnp.zeros((TILE, TILE), jnp.bfloat16)
             ttiles[tpd] = jnp.zeros((TILE, TILE), jnp.bfloat16)
-            load.wait()
-            make_transposed(0, tpd // 2)
             pl.semaphore_wait(barrier, len(greeted))
         for dz in reversed(ORDER[nz][1:]):
             send(zb.at[inst, 0], zb.at[inst, dz * nx], zb_send.at[inst], zb_z.at[inst, dz], z_peer(dz))
@@ -212,6 +227,7 @@
             outp[piece] = jnp.zeros((sides, PIECE), jnp.float32)
         if first:
             make_index()
+            load.wait()
         for dz in ORDER[nz][1:]:
             take(zb.at[inst, dz * nx], zb_z.at[inst, dz])
             for dx in reversed(ORDER[nx][1:]):
@@ -225,87 +241,146 @@
         if first:
             squares = norm_finish(0, squares, "z")
             norm_start(1, squares, "x")
-            make_transposed(tpd // 2, tpd)
+
+        def add(dz, steps, k):
+            origin = lax.rem(zh - dz + nz, nz) * nx
+            total = None
+            for dx in steps:
+                block = origin + lax.rem(x - dx + nx, nx)
+                product = dot(zb[inst, dz * nx + dx], tiles[idx_s[0, block * cbg + k]])
+                total = product if total is None else total + product
+            return total
 
         def group(i, carry):
             dz = order(i)
             take(zb.at[inst, pl.ds(dz * nx + 1, nx - 1)], zb_x.at[inst, dz])
-            origin = lax.rem(zh - dz + nz, nz) * nx
             for k in range(cbg):
-                total = None
-                for dx in range(nx):
-                    block = origin + lax.rem(x - dx + nx, nx)
-                    product = dot(zb[inst, dz * nx + dx], tiles[idx_s[0, block * cbg + k]])
-                    total = product if total is None else total + product
+                total = add(dz, range(nx), k)
                 outp[2 * k] += total[:, :PIECE]
                 outp[2 * k + 1] += total[:, PIECE:]
             return carry
 
         lax.fori_loop(0, nz - 1, group, 0)
+        last = ORDER[nz][-1]
+        for k in range(cbg):
+            total = add(last, [0], k)
+            outp[2 * k] += total[:, :PIECE]
+            outp[2 * k + 1] += total[:, PIECE:]
         squares = norm_finish(1, squares, "x") if first else norm_finish(3, squares, "row")
         n = 2 if first else 4
         norm_start(n, squares, "col")
-        group(nz - 1, 0)
-        for d in sorted(range(1, nc), key=lambda d: -min(d, nc - d)):
-            peer = lax.rem(c + d, nc)
-            csend[inst, d] = outp[peer].astype(jnp.bfloat16)
-            send(csend.at[inst, d], crecv.at[inst, d], c_send.at[inst], c_sem.at[inst], (r, peer))
+        take(zb.at[inst, pl.ds(last * nx + 1, nx - 1)], zb_x.at[inst, last])
+        for some in batches(chips[::-1], BACK_BATCH):
+            ready = []
+            for offset in some:
+                k = chip_at(offset, 1)
+                total = add(last, range(1, nx), k)
+                for h in range(2):
+                    value = outp[2 * k + h] + total[:, h * PIECE : (h + 1) * PIECE]
+                    slot = slot_of(offset)
+                    if any(offset):
+                        csend[inst, slot + h] = value.astype(jnp.bfloat16)
+                        ready.append((slot, h, 2 * k + h))
+                    else:
+                        outp[2 * k + h] = value
+            for slot, h, piece in ready:
+                send(
+                    csend.at[inst, slot + h],
+                    crecv.at[inst, slot + core],
+                    c_send.at[inst],
+                    c_sem.at[inst],
+                    (r, piece),
+                )
+        csend[inst, 0] = outp[c + 1 - 2 * core].astype(jnp.bfloat16)
+        send(
+            csend.at[inst, 0],
+            crecv.at[inst, core],
+            c_send.at[inst],
+            c_sem.at[inst],
+            (r, c + 1 - 2 * core),
+        )
+        if first:
+            make_transposed(0, tpd)
         squares = norm_finish(n, squares, "col")
         norm = jnp.sqrt(to_column(squares) + EPSILON)
         prepared = prepare(norm)
         take(crecv.at[inst, pl.ds(1, nc - 1)], c_sem.at[inst])
-        total = outp[c]
-        for d in range(1, nc):
-            total = total + crecv[inst, d].astype(jnp.float32)
+        total = outp[c] + crecv[inst, 1 - core].astype(jnp.float32)
+        for slot in range(2, nc):
+            total = total + crecv[inst, slot].astype(jnp.float32)
         return total, norm, prepared
 
     def forward(inst, vector, n, prepare):
-        wrecv[inst, 0] = vector.astype(jnp.bfloat16)
-        for d in sorted(range(1, nc), key=lambda d: -min(d, nc - d)):
-            send(
-                wrecv.at[inst, 0],
-                wrecv.at[inst, d],
-                w_send.at[inst],
-                w_sem.at[inst],
-                (r, lax.rem(c + d, nc)),
-            )
+        wrecv[inst, core] = vector.astype(jnp.bfloat16)
+        for offset in reversed(chips):
+            slot = slot_of(offset)
+            chip = chip_at(offset, 1)
+            targets = [2 * chip, 2 * chip + 1] if any(offset) else [c + 1 - 2 * core]
+            for target in targets:
+                send(
+                    wrecv.at[inst, core],
+                    wrecv.at[inst, slot + core],
+                    w_send.at[inst],
+                    w_sem.at[inst, slot // 2],
+                    (r, target),
+                )
         squares = square_sum(vector)
         norm_start(n, squares, "col")
-        take(wrecv.at[inst, pl.ds(1, nc - 1)], w_sem.at[inst])
-        for k in range(cbg):
-            wfull[k, :, :PIECE] = wrecv[inst, lax.rem(c - 2 * k + nc, nc)]
-            wfull[k, :, PIECE:] = wrecv[inst, lax.rem(c - 2 * k - 1 + nc, nc)]
-
-        def group(i, carry):
-            dz = order(nz - 1 - i)
-            for dx in reversed(ORDER[nx]):
-                block = lax.rem(zh + dz, nz) * nx + lax.rem(x + dx, nx)
-                total = None
-                for k in range(cbg):
-                    product = dot(wfull[k], ttiles[idx_s[0, block * cbg + k]])
-                    total = product if total is None else total + product
-                if dx == 0:
-                    part[dz] = total
+
+        def arrive(offset):
+            slot = slot_of(offset)
+            if any(offset):
+                take(wrecv.at[inst, pl.ds(slot, 2)], w_sem.at[inst, slot // 2])
+            else:
+                take(wrecv.at[inst, pl.ds(1 - core, 1)], w_sem.at[inst, 0])
+            wfull[slot // 2, :, :PIECE] = wrecv[inst, slot]
+            wfull[slot // 2, :, PIECE:] = wrecv[inst, slot + 1]
+
+        def add(block, offsets):
+            total = None
+            for offset in offsets:
+                k = chip_at(offset, -1)
+                product = dot(wfull[slot_of(offset) // 2], ttiles[idx_s[0, block * cbg + k]])
+                total = product if total is None else total + product
+            return total
+
+        def block_at(dz, dx):
+            return lax.rem(zh + dz, nz) * nx + lax.rem(x + dx, nx)
+
+        stages = [chips[s : s + 2] for s in range(0, len(chips), 2)]
+        for s, offsets in enumerate(stages[:-1]):
+            for offset in offsets:
+                arrive(offset)
+            for slot in range(nr):
+                total = add(block_at(slot // nx, slot % nx), offsets)
+                part[slot] = total if s == 0 else part[slot] + total
+        squares = norm_finish(n, squares, "col")
+        norm_start(n + 1, squares, "row")
+        for offset in stages[-1]:
+            arrive(offset)
+        slots = [dz * nx + dx for dz in reversed(ORDER[nz]) for dx in reversed(ORDER[nx])]
+        for some in batches(slots, FORWARD_BATCH):
+            for slot in some:
+                total = add(block_at(slot // nx, slot % nx), stages[-1])
+                if len(stages) > 1:
+                    total = part[slot] + total
+                if slot % nx == 0:
+                    part[slot] = total
                 else:
-                    slot = dz * nx + dx
                     s1send[inst, slot] = total.astype(jnp.bfloat16)
+            for slot in some:
+                if slot % nx:
                     send(
                         s1send.at[inst, slot],
                         s1recv.at[inst, slot],
                         s1_send.at[inst],
-                        s1_sem.at[inst, dz],
-                        x_peer(dx),
+                        s1_sem.at[inst, slot // nx],
+                        x_peer(slot % nx),
                     )
-            return carry
-
-        group(0, 0)
-        squares = norm_finish(n, squares, "col")
-        norm_start(n + 1, squares, "row")
-        lax.fori_loop(1, nz, group, 0)
         total = None
         for dz in reversed(ORDER[nz]):
             take(s1recv.at[inst, pl.ds(dz * nx + 1, nx - 1)], s1_sem.at[inst, dz])
-            total = part[dz]
+            total = part[dz * nx]
             for dx in range(1, nx):
                 total = total + s1recv[inst, dz * nx + dx].astype(jnp.float32)
             if dz:
@@ -412,7 +487,7 @@
             pltpu.VMEM((2, nr, sides, TILE), bf16),
             pltpu.VMEM((2, nz, sides, TILE), bf16),
             pltpu.VMEM((2, nz, sides, TILE), bf16),
-            pltpu.VMEM((nz, sides, TILE), f32),
+            pltpu.VMEM((nr, sides, TILE), f32),
             pltpu.VMEM((2, nc, sides, PIECE), bf16),
             pltpu.VMEM((2, nc, sides, PIECE), bf16),
             pltpu.VMEM((2, nc, sides, PIECE), bf16),
@@ -436,7 +511,7 @@
             dma((2,)),
             dma((2,)),
             dma((2,)),
-            dma((2,)),
+            dma((2, cbg)),
             dma((11,)),
             dma((11,)),
         ],

time: 93.8 us -> 91.8 us (0.979)
  Pallas kernels: 92.3 us -> 90.4 us
    pallas_call x1, Pallas kernels: 90.8 us -> 88.9 us  [local(): pl.pallas_call(functools.partial(kernel, dims), out_shape=(jax.ShapeDtype...]
where the time goes in v3:
time: 91.8 us; the launch traced here: 91.7 us
  Pallas kernels  90.4 us (98%)
  between operations  1.29 us (1%)
    pallas_call x1, Pallas kernels, local(): pl.pallas_call(functools.partial(kernel, dims), out_shape=(jax.ShapeDtype...  88.9 us

profile of v3, /device:TPU:1, one launch (start us, length us, event | category | flops | bytes accessed | tf_op | source)
XLA Modules:
  0.0 91.7 jit_solution(6180646462305569171)
XLA Ops:
  1.3 88.9 %lsqr.1 = (f32[64,128]{1,0:T(8,128)}, f32[64,256]{1,0:T(8,128)}) custom-call(s32[1,1,64]{2,1,0:T(1,128)} %rows_hbm.1, s32[1,1,64]{2,1,0:T(1,128)} %cols_hbm.1, s32[1,1]{1,0:T(1,128)S(6)} %copy.7.count_hbm, f32[64,1,256]{2,1,0:T(1,128)} %rhs_hbm.1, bf16[1,1,64,256,256]{4,3,2,1,0:T(8,128)(2,1)} %tiles_hbm.1), custom_call_target="tpu_custom_call" | custom-call | tf_op jit(solution)/shard_map/lsqr/pallas_call | solution.py:468
  90.2 1.5 %place.1 = (f32[64,1,128]{2,1,0:T(1,128)}, f32[64,1,256]{2,1,0:T(1,128)}) custom-call(f32[64,128]{1,0:T(8,128)} %get-tuple-element.4.solution, f32[64,256]{1,0:T(8,128)} %get-tuple-element.5.residual), custom_call_target="tpu_custom_call" | custom-call | tf_op jit(solution)/shard_map/place/pallas_call | solution.py:523

commit v4 on v3

--- a/solution.py
+++ b/solution.py
@@ -90,7 +90,6 @@
     x = lax.rem(r, nx)
 
     load = pltpu.make_async_copy(tiles_hbm.at[0, 0], tiles.at[pl.ds(0, tpd)], tile_sem)
-    load.start()
     small = [
         pltpu.make_async_copy(rows_hbm, rows_s, small_sem.at[0]),
         pltpu.make_async_copy(cols_hbm, cols_s, small_sem.at[1]),
@@ -99,6 +98,8 @@
     ]
     for copy in small:
         copy.start()
+
+    load.start()
 
     barrier = pltpu.get_barrier_semaphore()
 
@@ -336,9 +337,9 @@
             wfull[slot // 2, :, :PIECE] = wrecv[inst, slot]
             wfull[slot // 2, :, PIECE:] = wrecv[inst, slot + 1]
 
-        def add(block, offsets):
+        def add(block):
             total = None
-            for offset in offsets:
+            for offset in chips:
                 k = chip_at(offset, -1)
                 product = dot(wfull[slot_of(offset) // 2], ttiles[idx_s[0, block * cbg + k]])
                 total = product if total is None else total + product
@@ -347,25 +348,14 @@
         def block_at(dz, dx):
             return lax.rem(zh + dz, nz) * nx + lax.rem(x + dx, nx)
 
-        stages = [chips[s : s + 2] for s in range(0, len(chips), 2)]
-        for s, offsets in enumerate(stages[:-1]):
-            for offset in offsets:
-                arrive(offset)
-            for slot in range(nr):
-                total = add(block_at(slot // nx, slot % nx), offsets)
-                part[slot] = total if s == 0 else part[slot] + total
-        squares = norm_finish(n, squares, "col")
-        norm_start(n + 1, squares, "row")
-        for offset in stages[-1]:
+        for offset in chips:
             arrive(offset)
         slots = [dz * nx + dx for dz in reversed(ORDER[nz]) for dx in reversed(ORDER[nx])]
         for some in batches(slots, FORWARD_BATCH):
             for slot in some:
-                total = add(block_at(slot // nx, slot % nx), stages[-1])
-                if len(stages) > 1:
-                    total = part[slot] + total
+                total = add(block_at(slot // nx, slot % nx))
                 if slot % nx == 0:
-                    part[slot] = total
+                    part[slot // nx] = total
                 else:
                     s1send[inst, slot] = total.astype(jnp.bfloat16)
             for slot in some:
@@ -377,10 +367,12 @@
                         s1_sem.at[inst, slot // nx],
                         x_peer(slot % nx),
                     )
+        squares = norm_finish(n, squares, "col")
+        norm_start(n + 1, squares, "row")
         total = None
         for dz in reversed(ORDER[nz]):
             take(s1recv.at[inst, pl.ds(dz * nx + 1, nx - 1)], s1_sem.at[inst, dz])
-            total = part[dz * nx]
+            total = part[dz]
             for dx in range(1, nx):
                 total = total + s1recv[inst, dz * nx + dx].astype(jnp.float32)
             if dz:
@@ -487,7 +479,7 @@
             pltpu.VMEM((2, nr, sides, TILE), bf16),
             pltpu.VMEM((2, nz, sides, TILE), bf16),
             pltpu.VMEM((2, nz, sides, TILE), bf16),
-            pltpu.VMEM((nr, sides, TILE), f32),
+            pltpu.VMEM((nz, sides, TILE), f32),
             pltpu.VMEM((2, nc, sides, PIECE), bf16),
             pltpu.VMEM((2, nc, sides, PIECE), bf16),
             pltpu.VMEM((2, nc, sides, PIECE), bf16),

time: 91.8 us -> 88 us (0.959)
  Pallas kernels: 90.4 us -> 86.6 us
    pallas_call x1, Pallas kernels: 88.9 us -> 85 us  [local(): pl.pallas_call(functools.partial(kernel, dims), out_shape=(jax.ShapeDtype...]
where the time goes in v4:
time: 88 us; the launch traced here: 87.9 us
  Pallas kernels  86.6 us (98%)
  between operations  1.29 us (1%)
    pallas_call x1, Pallas kernels, local(): pl.pallas_call(functools.partial(kernel, dims), out_shape=(jax.ShapeDtype...  85 us

profile of v4, /device:TPU:1, one launch (start us, length us, event | category | flops | bytes accessed | tf_op | source)
XLA Modules:
  0.0 87.9 jit_solution(11575582460403083709)
XLA Ops:
  1.3 85.0 %lsqr.1 = (f32[64,128]{1,0:T(8,128)}, f32[64,256]{1,0:T(8,128)}) custom-call(s32[1,1,64]{2,1,0:T(1,128)} %rows_hbm.1, s32[1,1,64]{2,1,0:T(1,128)} %cols_hbm.1, s32[1,1]{1,0:T(1,128)S(6)} %copy.7.count_hbm, f32[64,1,256]{2,1,0:T(1,128)} %rhs_hbm.1, bf16[1,1,64,256,256]{4,3,2,1,0:T(8,128)(2,1)} %tiles_hbm.1), custom_call_target="tpu_custom_call" | custom-call | tf_op jit(solution)/shard_map/lsqr/pallas_call | solution.py:460
  86.3 1.5 %place.1 = (f32[64,1,128]{2,1,0:T(1,128)}, f32[64,1,256]{2,1,0:T(1,128)}) custom-call(f32[64,128]{1,0:T(8,128)} %get-tuple-element.4.solution, f32[64,256]{1,0:T(8,128)} %get-tuple-element.5.residual), custom_call_target="tpu_custom_call" | custom-call | tf_op jit(solution)/shard_map/place/pallas_call | solution.py:515

commit v5 on v4

--- a/solution.py
+++ b/solution.py
@@ -215,8 +215,16 @@
             tiles[tpd] = jnp.zeros((TILE, TILE), jnp.bfloat16)
             ttiles[tpd] = jnp.zeros((TILE, TILE), jnp.bfloat16)
             pl.semaphore_wait(barrier, len(greeted))
-        for dz in reversed(ORDER[nz][1:]):
-            send(zb.at[inst, 0], zb.at[inst, dz * nx], zb_send.at[inst], zb_z.at[inst, dz], z_peer(dz))
+        halves = [pl.ds(h * (sides // 2), sides // 2) for h in range(2)]
+        for h, rows in enumerate(halves):
+            for dz in reversed(ORDER[nz][1:]):
+                send(
+                    zb.at[inst, 0, rows],
+                    zb.at[inst, dz * nx, rows],
+                    zb_send.at[inst],
+                    zb_z.at[inst, dz, h],
+                    z_peer(dz),
+                )
         for dx in reversed(ORDER[nx][1:]):
             send(zb.at[inst, 0], zb.at[inst, dx], zb_send.at[inst], zb_x.at[inst, 0], x_peer(dx))
         if first:
@@ -230,15 +238,16 @@
             make_index()
             load.wait()
         for dz in ORDER[nz][1:]:
-            take(zb.at[inst, dz * nx], zb_z.at[inst, dz])
-            for dx in reversed(ORDER[nx][1:]):
-                send(
-                    zb.at[inst, dz * nx],
-                    zb.at[inst, dz * nx + dx],
-                    zb_send.at[inst],
-                    zb_x.at[inst, dz],
-                    x_peer(dx),
-                )
+            for h, rows in enumerate(halves):
+                take(zb.at[inst, dz * nx, rows], zb_z.at[inst, dz, h])
+                for dx in reversed(ORDER[nx][1:]):
+                    send(
+                        zb.at[inst, dz * nx, rows],
+                        zb.at[inst, dz * nx + dx, rows],
+                        zb_send.at[inst],
+                        zb_x.at[inst, dz],
+                        x_peer(dx),
+                    )
         if first:
             squares = norm_finish(0, squares, "z")
             norm_start(1, squares, "x")
@@ -494,7 +503,7 @@
             dma,
             dma,
             dma((2,)),
-            dma((2, nz)),
+            dma((2, nz, 2)),
             dma((2, nz)),
             dma((2,)),
             dma((2, nz)),

time: 88 us -> 88.1 us (level)
  no operation moved by 1% of the time
where the time goes in v5:
time: 88.1 us; the launch traced here: 87.9 us
  Pallas kernels  86.6 us (98%)
  between operations  1.29 us (1%)
    pallas_call x1, Pallas kernels, local(): pl.pallas_call(functools.partial(kernel, dims), out_shape=(jax.ShapeDtype...  85.1 us

profile of v5, /device:TPU:1, one launch (start us, length us, event | category | flops | bytes accessed | tf_op | source)
XLA Modules:
  0.0 87.9 jit_solution(8638026972388674015)
XLA Ops:
  1.3 85.1 %lsqr.1 = (f32[64,128]{1,0:T(8,128)}, f32[64,256]{1,0:T(8,128)}) custom-call(s32[1,1,64]{2,1,0:T(1,128)} %rows_hbm.1, s32[1,1,64]{2,1,0:T(1,128)} %cols_hbm.1, s32[1,1]{1,0:T(1,128)S(6)} %copy.7.count_hbm, f32[64,1,256]{2,1,0:T(1,128)} %rhs_hbm.1, bf16[1,1,64,256,256]{4,3,2,1,0:T(8,128)(2,1)} %tiles_hbm.1), custom_call_target="tpu_custom_call" | custom-call | tf_op jit(solution)/shard_map/lsqr/pallas_call | solution.py:469
  86.4 1.5 %place.1 = (f32[64,1,128]{2,1,0:T(1,128)}, f32[64,1,256]{2,1,0:T(1,128)}) custom-call(f32[64,128]{1,0:T(8,128)} %get-tuple-element.4.solution, f32[64,256]{1,0:T(8,128)} %get-tuple-element.5.residual), custom_call_target="tpu_custom_call" | custom-call | tf_op jit(solution)/shard_map/place/pallas_call | solution.py:524
